TPU v7x, 256 devices: a whole 4x4x8 slice. The times are simulated.
256 devices in a mesh: ep: 16 (over y, z_lo), dp: 16 (over x, z_hi, core).
Axes of the slice: x: 4, y: 4, z: 8 (z_hi: 2, z_lo: 4; z = z_hi * 4 + z_lo), core: 2. Of those that a mesh axis runs over, the one named last changes fastest.
Arguments:
- tokens: bfloat16 [32768, 2048], P(('ep', 'dp')), may hold values from -6 to 6
- grad_out: bfloat16 [32768, 2048], P(('ep', 'dp')), may hold values from -6 to 6
- routes: int32 [32768, 8], P(('ep', 'dp')), may hold values from 0 to 31, all different within a row; in each aligned block of 128 rows (0 to 127, 128 to 255, ...) at most 40 rows name the same one
- probs: float32 [32768, 8], P(('ep', 'dp')), may hold values from 0.02 to 0.3
- old_place: int32 [32], replicated, may hold values from 0 to 31, as said below
- new_place: int32 [32], replicated, may hold values from 0 to 31, as said below
- gate_w: bfloat16 [32, 2048, 512], P('ep', 'dp'), may hold values from -0.125 to 0.125
- gate_m: bfloat16 [32, 2048, 512], P('ep', 'dp'), may hold values from -6 to 6
- gate_v: bfloat16 [32, 2048, 512], P('ep', 'dp'), may hold values from 0.5 to 8
- down_w: bfloat16 [32, 512, 2048], P('ep', None, 'dp'), may hold values from -0.25 to 0.25
- down_m: bfloat16 [32, 512, 2048], P('ep', None, 'dp'), may hold values from -6 to 6
- down_v: bfloat16 [32, 512, 2048], P('ep', None, 'dp'), may hold values from 0.5 to 8
Outputs:
- mixed: bfloat16 [32768, 2048], P(('ep', 'dp'))
- grad_tokens: bfloat16 [32768, 2048], P(('ep', 'dp'))
- grad_probs: float32 [32768, 8], P(('ep', 'dp'))
- gate_w_next: bfloat16 [32, 2048, 512], P('ep', 'dp')
- gate_m_next: bfloat16 [32, 2048, 512], P('ep', 'dp')
- gate_v_next: bfloat16 [32, 2048, 512], P('ep', 'dp')
- down_w_next: bfloat16 [32, 512, 2048], P('ep', None, 'dp')
- down_m_next: bfloat16 [32, 512, 2048], P('ep', None, 'dp')
- down_v_next: bfloat16 [32, 512, 2048], P('ep', None, 'dp')
Inputs may be any that keep to these rules, and one draw needn't show every extreme that they name: `old_place`: A permutation of the experts; slot s lies on ep rank s // 2. `new_place`: equal to old_place except in exactly 3 slots, one on each of the ep ranks r, r - 1 and r - 1 - 16 // 2 (modulo 16) for some r; the slot on rank r receives the expert of the slot on r - 1, that one the expert of the slot on r - 1 - 16 // 2, and that one the expert of the slot on r. `routes`: A row's 8 experts differ; in each aligned block of 128 rows (the rows of one device) no expert is named by more than 40 rows, and in some block one expert is named by exactly 40 rows.
All inputs are finite; a program needn't handle non-finite values.
Results may differ from a plain program's by a relative error of at most 0.025.
Values may be sent and summed in bfloat16 or wider, within the bound.
No kernel may reach another device: no remote copies, remote signals or barrier semaphores. Data moves between devices by JAX's collectives and lax.ppermute only.
A program may use at most 128 MiB of HBM per device.

v0:
```python
import jax
import jax.numpy as jnp
from jax import lax
from jax.sharding import PartitionSpec as P

MOVES = 3
MOST = 40


beta_one = 0.9
beta_two = 0.95
step_rate = 0.001
adam_eps = 1e-08


def from_root(block, axis, source):
    block = jnp.where(lax.axis_index(axis) == source, block, jnp.zeros_like(block))
    return lax.psum(block, axis)


def silu_slope(values):
    sigmoid = jax.nn.sigmoid(values)
    return sigmoid * (1.0 + values * (1.0 - sigmoid))


def adam_update(weight, first, second, grad):
    first_new = beta_one * first.astype(jnp.float32) + (1.0 - beta_one) * grad
    second_new = beta_two * second.astype(jnp.float32) + (1.0 - beta_two) * grad * grad
    weight_new = weight.astype(jnp.float32) - step_rate * first_new / (
        jnp.sqrt(second_new) + adam_eps
    )
    return (
        weight_new.astype(jnp.bfloat16),
        first_new.astype(jnp.bfloat16),
        second_new.astype(jnp.bfloat16),
    )


def per_device(
    tokens,
    grad_out,
    routes,
    probs,
    old_place,
    new_place,
    gate_w,
    gate_m,
    gate_v,
    down_w,
    down_m,
    down_v,
):
    tok_rows, width = tokens.shape
    choose_count = routes.shape[1]
    experts = old_place.shape[0]
    local_count = gate_w.shape[0]
    hidden_units = gate_w.shape[2]
    ep_size = lax.axis_size("ep")
    my_rank = lax.axis_index("ep")
    slot_ids = jnp.arange(experts, dtype=jnp.int32)
    local_ids = jnp.arange(local_count, dtype=jnp.int32)
    moving = (new_place != old_place).astype(jnp.int32)
    moving_order = jnp.cumsum(moving) - 1
    initials = (gate_w, gate_m, gate_v, down_w, down_m, down_v)
    current = initials
    for move_index in range(MOVES):
        target = jnp.sum(jnp.where((moving == 1) & (moving_order == move_index), slot_ids, 0))
        wanted = jnp.sum(jnp.where(slot_ids == target, new_place, 0))
        source = jnp.sum(jnp.where(old_place == wanted, slot_ids, 0))
        picked = [
            lax.dynamic_index_in_dim(state, source % local_count, 0, keepdims=False)
            for state in initials
        ]
        arrived = (
            from_root(picked[0], "ep", source // local_count),
            from_root(picked[1], "ep", source // local_count),
            from_root(picked[2], "ep", source // local_count),
            from_root(picked[3], "ep", source // local_count),
            from_root(picked[4], "ep", source // local_count),
            from_root(picked[5], "ep", source // local_count),
        )
        landing = (local_ids == target % local_count) & (my_rank == target // local_count)
        current = tuple(
            (
                jnp.where(landing[:, None, None], fresh[None], state)
                for state, fresh in zip(current, arrived)
            )
        )
    inverse_new = jnp.sum(
        jnp.where(new_place[None, :] == slot_ids[:, None], slot_ids[None, :], 0), axis=1
    )
    flat_routes = routes.reshape(-1)
    route_hits = (flat_routes[:, None] == slot_ids[None, :]).astype(jnp.int32)
    new_slot = jnp.sum(route_hits * inverse_new[None, :], axis=1)
    within = jnp.sum((jnp.cumsum(route_hits, axis=0) - 1) * route_hits, axis=1)
    position = new_slot % local_count * (ep_size * MOST) + new_slot // local_count * MOST + within
    capacity = experts * MOST
    assign_ids = jnp.arange(tok_rows * choose_count, dtype=jnp.int32)
    source_row = jnp.zeros((capacity,), jnp.int32).at[position].set(assign_ids)
    occupied = jnp.zeros((capacity,), jnp.bool_).at[position].set(True)
    token_index = source_row // choose_count
    packed_tokens = jnp.where(occupied[:, None], tokens[token_index], jnp.zeros((), jnp.bfloat16))
    packed_tokens = packed_tokens.reshape(local_count, ep_size, MOST, width)
    slot_probs = probs.reshape(-1)[source_row]
    packed_grads = jnp.where(
        occupied[:, None], slot_probs[:, None] * grad_out[token_index].astype(jnp.float32), 0.0
    )
    packed_grads = packed_grads.astype(jnp.bfloat16).reshape(local_count, ep_size, MOST, width)
    gathered = []
    contract_last = (((1,), (1,)), ((), ()))
    contract_first = (((0,), (0,)), ((), ()))

    def run_forward(sent_rows):
        saved = []
        outputs = []
        for local_index in range(local_count):
            gate_full, down_full = (
                lax.all_gather(current[0][local_index], "dp", axis=0, tiled=True),
                lax.all_gather(current[3][local_index], "dp", axis=1, tiled=True),
            )
            gathered.append((gate_full, down_full))
            inputs = sent_rows[local_index].reshape(ep_size * MOST, width)
            pre = jnp.dot(inputs, gate_full, preferred_element_type=jnp.float32)
            hidden = jax.nn.silu(pre).astype(jnp.bfloat16)
            result = jnp.dot(hidden, down_full, preferred_element_type=jnp.float32).astype(
                jnp.bfloat16
            )
            saved.append((inputs, pre, hidden))
            outputs.append(result.reshape(ep_size, MOST, width))
        return (saved, jnp.stack(outputs, axis=0))

    sent_rows = lax.all_to_all(packed_tokens, "ep", split_axis=1, concat_axis=1, tiled=True)
    saved, expert_out = run_forward(sent_rows)
    back_rows = lax.all_to_all(expert_out, "ep", split_axis=1, concat_axis=1, tiled=True)
    sent_grads = lax.all_to_all(packed_grads, "ep", split_axis=1, concat_axis=1, tiled=True)
    backs = []
    updates = []
    for local_index in range(local_count):
        inputs, pre, hidden = saved[local_index]
        gate_full, down_full = gathered[local_index]
        upstream = sent_grads[local_index].reshape(ep_size * MOST, width)
        d_hidden = lax.dot_general(
            upstream, down_full, contract_last, preferred_element_type=jnp.float32
        )
        d_pre = (d_hidden * silu_slope(pre)).astype(jnp.bfloat16)
        d_inputs = lax.dot_general(
            d_pre, gate_full, contract_last, preferred_element_type=jnp.float32
        ).astype(jnp.bfloat16)
        backs.append(d_inputs.reshape(ep_size, MOST, width))
        gate_part = lax.dot_general(
            inputs, d_pre, contract_first, preferred_element_type=jnp.float32
        )
        down_part = lax.dot_general(
            upstream, hidden, contract_first, preferred_element_type=jnp.float32
        )
        summed = lax.psum_scatter(
            jnp.concatenate([gate_part, down_part], axis=1).astype(jnp.bfloat16),
            "dp",
            scatter_dimension=0,
            tiled=True,
        ).astype(jnp.float32)
        gate_grad = summed[:, :hidden_units]
        down_grad = jnp.transpose(summed[:, hidden_units:])
        gate_new = adam_update(
            current[0][local_index], current[1][local_index], current[2][local_index], gate_grad
        )
        down_new = adam_update(
            current[3][local_index], current[4][local_index], current[5][local_index], down_grad
        )
        updates.append(gate_new + down_new)
    expert_back, updates = (jnp.stack(backs, axis=0), updates)
    back_grads = lax.all_to_all(expert_back, "ep", split_axis=1, concat_axis=1, tiled=True)
    out_rows = back_rows.reshape(capacity, width)[position].reshape(tok_rows, choose_count, width)
    grad_rows = back_grads.reshape(capacity, width)[position].reshape(tok_rows, choose_count, width)
    mixed = jnp.sum(probs[:, :, None] * out_rows.astype(jnp.float32), axis=1).astype(jnp.bfloat16)
    grad_tokens = jnp.sum(grad_rows.astype(jnp.float32), axis=1).astype(jnp.bfloat16)
    grad_probs = jnp.sum(
        grad_out[:, None, :].astype(jnp.float32) * out_rows.astype(jnp.float32), axis=2
    )
    stacked = [jnp.stack([entry[member] for entry in updates], axis=0) for member in range(6)]
    return (
        mixed,
        grad_tokens,
        grad_probs,
        stacked[0],
        stacked[1],
        stacked[2],
        stacked[3],
        stacked[4],
        stacked[5],
    )


def solution(mesh):
    in_specs = (
        P(("ep", "dp"), None),
        P(("ep", "dp"), None),
        P(("ep", "dp"), None),
        P(("ep", "dp"), None),
        P(),
        P(),
        P("ep", "dp", None),
        P("ep", "dp", None),
        P("ep", "dp", None),
        P("ep", None, "dp"),
        P("ep", None, "dp"),
        P("ep", None, "dp"),
    )
    out_specs = (
        P(("ep", "dp"), None),
        P(("ep", "dp"), None),
        P(("ep", "dp"), None),
        P("ep", "dp", None),
        P("ep", "dp", None),
        P("ep", "dp", None),
        P("ep", None, "dp"),
        P("ep", None, "dp"),
        P("ep", None, "dp"),
    )
    return jax.shard_map(
        per_device, mesh=mesh, in_specs=in_specs, out_specs=out_specs, check_vma=False
    )
```

profile of v0, /device:TPU:33, one launch (start us, length us, event | category | flops | bytes accessed | tf_op | source)
XLA Modules:
  0.0 952.9 jit_solution(7776065592931866621)
XLA Ops:
  8.2 9.0 reduce-window.19
  28.1 6.1 gather_fusion
  39.5 8.2 all-to-all-start
  75.6 214.8 %all-reduce.3.cloned.1.call-done = (bf16[512,128]{1,0:T(8,128)(2,1)}, bf16[512,128]{1,0:T(8,128)(2,1)}, bf16[512,128]{1,0:T(8,128)(2,1)}, bf16[128,512]{1,0:T(8,...) async-done(((bf16[512,128]{1,0:T(8,128)(2,1)}, ...) | async-done | bytes 2359312 | tf_op jit(solution)/shard_map/psum | solution.py:18
  302.2 6.2 gather_fusion.3
  313.8 6.2 fusion.1
  321.1 7.6 all-to-all-start.2
  335.4 45.6 %all-gather.9.cloned.1.call-done = bf16[1,2048,512]{1,2,0:T(8,128)(2,1)} async-done(((bf16[1,128,512]{1,2,0:T(8,128)(2,1)}), bf16[1,2048,512]{1,2,0:T(8,128)(2,1)}) %all-gather.9.cloned.1.call-update) | async-done | bytes 2097168 | tf_op jit(solution)/shard_map/all_gather | solution.py:118
  385.2 82.5 %all-to-all-done.2 = bf16[2,16,40,2048]{3,2,0,1:T(8,128)(2,1)} async-done(((bf16[2,16,40,2048]{3,2,0,1:T(8,128)(2,1)}), bf16[2,16,40,2048]{3,2,0,1:T(8,128)(2,1)}, u32[]{:S(2)}, u32[]{:S(2)}) %all-to-all-start.2) | async-done | bytes 5242912 | tf_op jit(solution)/shard_map/all_to_all | solution.py:135
  467.7 5.8 fusion.69
  482.0 37.3 %all-gather.13.cloned.1.call-done = bf16[1,2048,512]{1,2,0:T(8,128)(2,1)} async-done(((bf16[1,128,512]{1,2,0:T(8,128)(2,1)}), bf16[1,2048,512]{1,2,0:T(8,128)(2,1)}) %all-gather.13.cloned.1.call-update) | async-done | bytes 2097168 | tf_op jit(solution)/shard_map/all_gather | solution.py:118
  524.4 56.6 %all-gather.15.cloned.1.call-done = bf16[1,512,2048]{2,1,0:T(8,128)(2,1)} async-done(((bf16[1,512,128]{2,1,0:T(8,128)(2,1)}), bf16[1,512,2048]{2,1,0:T(8,128)(2,1)}) %all-gather.15.cloned.1.call-update) | async-done | bytes 2097168 | tf_op jit(solution)/shard_map/all_gather | solution.py:119
  590.5 5.4 all-to-all-start.3
  604.5 6.4 copy.159
  619.0 119.0 %all-to-all-done.3 = bf16[2,16,40,2048]{3,2,0,1:T(8,128)(2,1)} async-done(((bf16[2,16,40,2048]{3,2,0,1:T(8,128)(2,1)}), bf16[2,16,40,2048]{3,2,0,1:T(8,128)(2,1)}, u32[]{:S(2)}, u32[]{:S(2)}) %all-to-all-start.3) | async-done | bytes 5242912 | tf_op jit(solution)/shard_map/all_to_all | solution.py:172
  738.0 9.5 all-to-all-start.1
  755.3 6.6 copy.157
  763.7 124.9 %reduce-scatter.7.cloned.1.call-done = bf16[128,1024]{1,0:T(8,128)(2,1)} async-done(((bf16[2048,1024]{1,0:T(8,128)(2,1)}), bf16[128,1024]{1,0:T(8,128)(2,1)}) %reduce-scatter.7.cloned.1.call-update) | async-done | bytes 262160
  898.1 5.7 copy.144
  903.8 12.0 %gather_fusion.4 = bf16[1024,2048]{1,0:T(8,128)(2,1)} fusion(bf16[1280,2048]{1,0:T(8,128)(2,1)} %bitcast.268, s32[1024]{0:T(1024)S(1)} %broadcast_clamp_fusion), kind=kCustom, calls=%fused_computation.4 | custom fusion | bytes 8392704 | tf_op jit(solution)/shard_map/gather | solution.py:174
  915.8 5.9 bitcast_reduce_fusion
  921.7 5.7 copy.138
  927.3 12.1 %gather_fusion.1 = bf16[1024,2048]{1,0:T(8,128)(2,1)} fusion(bf16[1280,2048]{1,0:T(8,128)(2,1)} %bitcast.267, s32[1024]{0:T(1024)S(1)} %broadcast_clamp_fusion), kind=kCustom, calls=%fused_computation.1 | custom fusion | bytes 8392704 | tf_op jit(solution)/shard_map/gather | solution.py:173
  939.4 5.7 fusion.3
  (197 shorter events, 117.1 us)
Async XLA Ops:
  7.2 20.9 %copy-start = (bf16[128,2048]{1,0:T(8,128)(2,1)S(1)}, bf16[128,2048]{1,0:T(8,128)(2,1)}, u32[]{:S(2)}) copy-start(bf16[128,2048]{1,0:T(8,128)(2,1)} %param.12) | copy-start | bytes 1572868
  18.6 15.6 %copy-start.28 = (s32[1024,1]{0,1:T(1,128)}, s32[1024,1]{0,1:T(1,128)S(1)}, u32[]{:S(2)}) copy-start(s32[1024,1]{0,1:T(1,128)S(1)} %compare_select_fusion) | copy-start | bytes 12292
  39.5 8.3 copy-start.35
  39.5 22.5 %copy-start.8 = (bf16[2,128,512]{2,1,0:T(8,128)(2,1)S(1)}, bf16[2,128,512]{2,1,0:T(8,128)(2,1)}, u32[]{:S(2)}) copy-start(bf16[2,128,512]{2,1,0:T(8,128)(2,1)} %param.18) | copy-start | bytes 786436
  39.5 23.3 %copy-start.11 = (bf16[2,512,128]{2,1,0:T(8,128)(2,1)S(1)}, bf16[2,512,128]{2,1,0:T(8,128)(2,1)}, u32[]{:S(2)}) copy-start(bf16[2,512,128]{2,1,0:T(8,128)(2,1)} %param.21) | copy-start | bytes 786436
  39.5 24.0 %copy-start.12 = (bf16[2,512,128]{2,1,0:T(8,128)(2,1)S(1)}, bf16[2,512,128]{2,1,0:T(8,128)(2,1)}, u32[]{:S(2)}) copy-start(bf16[2,512,128]{2,1,0:T(8,128)(2,1)} %param.23) | copy-start | bytes 786436
  39.5 24.0 %copy-start.13 = (bf16[2,512,128]{2,1,0:T(8,128)(2,1)S(1)}, bf16[2,512,128]{2,1,0:T(8,128)(2,1)}, u32[]{:S(2)}) copy-start(bf16[2,512,128]{2,1,0:T(8,128)(2,1)} %param.22) | copy-start | bytes 786436
  39.5 281.6 %all-to-all-start = ((bf16[2,16,40,2048]{3,2,0,1:T(8,128)(2,1)}), bf16[2,16,40,2048]{3,2,0,1:T(8,128)(2,1)}, u32[]{:S(2)}, u32[]{:S(2)}) async-start(bf16[2,16,40,2048]{3,2,0,1:T(8,128)(2,1)} %copy_select_fusion), calls=%async_computation | async-start | bytes 10485760 | tf_op jit(solution)/shard_map/all_to_all | solution.py:132
  47.7 16.7 %copy-start.9 = (bf16[2,128,512]{2,1,0:T(8,128)(2,1)S(1)}, bf16[2,128,512]{2,1,0:T(8,128)(2,1)}, u32[]{:S(2)}) copy-start(bf16[2,128,512]{2,1,0:T(8,128)(2,1)} %param.19) | copy-start | bytes 786436
  47.7 16.7 %copy-start.10 = (bf16[2,128,512]{2,1,0:T(8,128)(2,1)S(1)}, bf16[2,128,512]{2,1,0:T(8,128)(2,1)}, u32[]{:S(2)}) copy-start(bf16[2,128,512]{2,1,0:T(8,128)(2,1)} %param.20) | copy-start | bytes 786436
  47.8 242.7 %all-reduce.3.cloned.1.call-start = ((), (), s32[]{:S(2)}) async-start(), calls=%async_computation.12 | async-start | bytes 4718592 | tf_op jit(solution)/shard_map/psum | solution.py:18
  65.3 315.6 %all-gather.9.cloned.1.call-start = ((), (), s32[]{:S(2)}) async-start(), calls=%async_computation.6 | async-start | bytes 2228224 | tf_op jit(solution)/shard_map/all_gather | solution.py:118
  292.5 9.7 %copy-start.2 = (bf16[128,2048]{1,0:T(8,128)(2,1)S(1)}, bf16[128,2048]{1,0:T(8,128)(2,1)}, u32[]{:S(2)}) copy-start(bf16[128,2048]{1,0:T(8,128)(2,1)} %param.13) | copy-start | bytes 1572868
  321.1 146.6 %all-to-all-start.2 = ((bf16[2,16,40,2048]{3,2,0,1:T(8,128)(2,1)}), bf16[2,16,40,2048]{3,2,0,1:T(8,128)(2,1)}, u32[]{:S(2)}, u32[]{:S(2)}) async-start(bf16[2,16,40,2048]{3,2,0,1:T(8,128)(2,1)} %fusion.1), calls=%async_computation.2 | async-start | bytes 10485760 | tf_op jit(solution)/shard_map/all_to_all | solution.py:135
  328.7 144.8 %all-gather.11.cloned.1.call-start = ((), (), s32[]{:S(2)}) async-start(), calls=%async_computation.7 | async-start | bytes 2228224 | tf_op jit(solution)/shard_map/all_gather | solution.py:119
  329.5 189.8 %all-gather.13.cloned.1.call-start = ((), (), s32[]{:S(2)}) async-start(), calls=%async_computation.8 | async-start | bytes 2228224 | tf_op jit(solution)/shard_map/all_gather | solution.py:118
  330.1 250.9 %all-gather.15.cloned.1.call-start = ((), (), s32[]{:S(2)}) async-start(), calls=%async_computation.9 | async-start | bytes 2228224 | tf_op jit(solution)/shard_map/all_gather | solution.py:119
  590.5 147.5 %all-to-all-start.3 = ((bf16[2,16,40,2048]{3,2,0,1:T(8,128)(2,1)}), bf16[2,16,40,2048]{3,2,0,1:T(8,128)(2,1)}, u32[]{:S(2)}, u32[]{:S(2)}) async-start(bf16[2,16,40,2048]{3,2,0,1:T(8,128)(2,1)} %pad_maximum_fusion.1), calls=%async_computation.3 | async-start | bytes 10485760 | tf_op jit(solution)/shard_map/all_to_all | solution.py:172
  595.9 166.7 %reduce-scatter.9.cloned.1.call-start = ((), (), s32[]{:S(2)}) async-start(), calls=%async_computation.11 | async-start | bytes 4456448
  738.0 183.7 %all-to-all-start.1 = ((bf16[2,16,40,2048]{3,2,0,1:T(8,128)(2,1)}), bf16[2,16,40,2048]{3,2,0,1:T(8,128)(2,1)}, u32[]{:S(2)}, u32[]{:S(2)}) async-start(bf16[2,16,40,2048]{3,2,0,1:T(8,128)(2,1)} %pad_maximum_fusion), calls=%async_computation.1 | async-start | bytes 10485760 | tf_op jit(solution)/shard_map/all_to_all | solution.py:134
  747.5 141.1 %reduce-scatter.7.cloned.1.call-start = ((), (), s32[]{:S(2)}) async-start(), calls=%async_computation.10 | async-start | bytes 4456448
  761.9 127.9 %copy-start.14 = (bf16[2,128,512]{1,2,0:T(8,128)(2,1)S(1)}, bf16[2,128,512]{1,2,0:T(8,128)(2,1)}, u32[]{:S(2)}) copy-start(bf16[2,128,512]{1,2,0:T(8,128)(2,1)} %get-tuple-element.131) | copy-start | bytes 786436
  761.9 127.9 %copy-start.15 = (bf16[2,128,512]{1,2,0:T(8,128)(2,1)S(1)}, bf16[2,128,512]{1,2,0:T(8,128)(2,1)}, u32[]{:S(2)}) copy-start(bf16[2,128,512]{1,2,0:T(8,128)(2,1)} %get-tuple-element.132) | copy-start | bytes 786436
  927.3 18.4 %copy-start.1 = (bf16[128,2048]{1,0:T(8,128)(2,1)S(1)}, bf16[128,2048]{1,0:T(8,128)(2,1)}, u32[]{:S(2)}) copy-start(bf16[128,2048]{1,0:T(8,128)(2,1)} %param.12) | copy-start | bytes 1572868
  (31 other events, 156.2 us)
Sparse Core Ops, SparseCore 0:
  65.5 224.9 all-reduce.2
  302.3 78.6 all-gather.8
  384.1 68.9 all-gather.10
  455.5 63.7 all-gather.12
  522.3 58.6 all-gather.14
  611.0 126.0 reduce-scatter.8
  762.0 126.5 reduce-scatter.6
where the time goes:
time: 963 us; the launch traced here: 953 us
  waiting for transfers between devices  682 us (71%)
  local copies, waits for them, and re-layouts  105 us (11%)
  other arithmetic  63.9 us (7%)
  matrix products  39.2 us (4%)
  starting transfers between devices  31.6 us (3%)
  between operations  31.1 us (3%)
    psum x1, waiting for transfers between devices, from_root(): return lax.psum(block, axis)  215 us
    unnamed x9, waiting for transfers between devices  126 us
    all_to_all x1, waiting for transfers between devices, per_device(): lax.all_to_all(expert_back, 'ep', split_axis=1, concat_axis=1, tiled=True)  119 us
    all_gather x2, waiting for transfers between devices, run_forward(): lax.all_gather(current[0][local_index], 'dp', axis=0, tiled=True)  82.9 us
    all_to_all x1, waiting for transfers between devices, per_device(): lax.all_to_all(packed_grads, 'ep', split_axis=1, concat_axis=1, tiled=True)  82.5 us
    all_gather x2, waiting for transfers between devices, run_forward(): lax.all_gather(current[3][local_index], 'dp', axis=1, tiled=True)  56.6 us
    unnamed x101, local copies, waits for them, and re-layouts  21.9 us
  transfers between devices with their start and end apart: 11, of which 7 were waited for; matrix products, arithmetic and copies ran while one was open for 15% of the time, Pallas kernels for 0%

commit v1 on v0

v1 whole, which is shorter than its diff:
```python
import jax
import jax.numpy as jnp
from jax import lax
from jax.sharding import PartitionSpec as P

beta_one = 0.9
beta_two = 0.95
step_rate = 0.001
adam_eps = 1e-08

BOTH = ("ep", "dp")
N_Y, N_ZL, N_X, N_ZH, N_C = 4, 4, 4, 2, 2
N_EP, N_DP = N_Y * N_ZL, N_X * N_ZH * N_C
F32, BF16 = jnp.float32, jnp.bfloat16


def links(move):
    pairs = []
    for ep in range(N_EP):
        for dp in range(N_DP):
            y, zl = divmod(ep, N_ZL)
            x, rest = divmod(dp, N_ZH * N_C)
            zh, c = divmod(rest, N_C)
            y, x, z, c = move(y, x, zh * N_ZL + zl, c)
            zh, zl = divmod(z % (N_ZH * N_ZL), N_ZL)
            there = (y % N_Y * N_ZL + zl) * N_DP + x % N_X * N_ZH * N_C + zh * N_C + c
            pairs.append((ep * N_DP + dp, there))
    return pairs


Y_UP = links(lambda y, x, z, c: (y + 1, x, z, c))
Y_DOWN = links(lambda y, x, z, c: (y - 1, x, z, c))
X_UP = links(lambda y, x, z, c: (y, x + 1, z, c))
X_DOWN = links(lambda y, x, z, c: (y, x - 1, z, c))
Z_UP = links(lambda y, x, z, c: (y, x, z + 2, c))
Z_DOWN = links(lambda y, x, z, c: (y, x, z - 2, c))
Z_PAIR = links(lambda y, x, z, c: (y, x, z ^ 1, c))
CORE = links(lambda y, x, z, c: (y, x, z, 1 - c))


def send(block, pairs):
    return lax.ppermute(block, BOTH, pairs)


def spread(block, up, down):
    half = block.shape[0] // 2
    left, right = send(block, up), send(block, down)
    far = [send(left[:half], up), send(right[half:], down)]
    return [block, left, right] + far


def collect(blocks, up, down):
    own, left, right, far = blocks
    half = far.shape[0] // 2
    from_left, from_right = send(far[:half], up), send(far[half:], down)
    right = jnp.concatenate([add(right[:half], from_left), right[half:]], axis=0)
    left = jnp.concatenate([left[:half], add(left[half:], from_right)], axis=0)
    return own, send(right, up), send(left, down)


def add(first, second):
    return (first.astype(F32) + second.astype(F32)).astype(BF16)


def choose(index, options):
    picked = options[0]
    for number in range(1, len(options)):
        picked = jnp.where(index == number, options[number], picked)
    return picked


def to_relative(rows, x, zh, c):
    width = rows.shape[1] // N_DP
    part = lambda i, j, k: rows[:, ((i * N_ZH + j) * N_C + k) * width :][:, :width]
    cols = []
    for j in range(N_ZH):
        for k in range(N_C):
            for step in (0, -1, 1, 2):
                by_x = []
                for i in range(N_X):
                    source = (i + step) % N_X
                    by_x.append(
                        choose(zh * N_C + c, [part(source, j ^ (n // N_C), k ^ (n % N_C)) for n in range(4)])
                    )
                cols.append(choose(x, by_x))
    return jnp.concatenate(cols, axis=1)


def to_absolute(rows, x, zh, c):
    width = rows.shape[1] // N_DP
    place = {0: 0, 3: 1, 1: 2, 2: 3}
    part = lambda j, k, step: rows[:, ((j * N_C + k) * N_X + place[step % N_X]) * width :][:, :width]
    cols = []
    for i in range(N_X):
        for j in range(N_ZH):
            for k in range(N_C):
                by_x = [
                    choose(zh * N_C + c, [part(j ^ (n // N_C), k ^ (n % N_C), i - here) for n in range(4)])
                    for here in range(N_X)
                ]
                cols.append(choose(x, by_x))
    return jnp.concatenate(cols, axis=1)


def adam_update(weight, first, second, grad):
    first_new = beta_one * first.astype(F32) + (1.0 - beta_one) * grad
    second_new = beta_two * second.astype(F32) + (1.0 - beta_two) * grad * grad
    weight_new = weight.astype(F32) - step_rate * first_new / (jnp.sqrt(second_new) + adam_eps)
    return weight_new.astype(BF16), first_new.astype(BF16), second_new.astype(BF16)


def dot(left, right, dims=((1,), (0,))):
    return lax.dot_general(left, right, (dims, ((), ())), preferred_element_type=F32)


ROWS = ((0,), (0,))
COLS = ((1,), (1,))


def per_device(tokens, grad_out, routes, probs, old_place, new_place, gate_w, gate_m, gate_v, down_w, down_m, down_v):
    tok_rows, width = tokens.shape
    choose_count = routes.shape[1]
    experts = old_place.shape[0]
    local_count, shard, hidden = gate_w.shape
    ep, dp = lax.axis_index("ep"), lax.axis_index("dp")
    y, zl = ep // N_ZL, ep % N_ZL
    zb, za = zl // 2, zl % 2
    x, zh, c = dp // (N_ZH * N_C), dp // N_C % N_ZH, dp % N_C
    slots = jnp.arange(experts, dtype=jnp.int32)

    changed = new_place != old_place
    source = jnp.sum(jnp.where(new_place[:, None] == old_place[None, :], slots[None, :], 0), axis=1)
    first = changed & (source // local_count == (slots // local_count - 1) % N_EP)
    root = jnp.sum(jnp.where(first, slots // local_count, 0))
    mine = lax.dynamic_slice_in_dim(changed, ep * local_count, local_count)
    moved = mine[1:].astype(jnp.int32).sum()

    def side(state):
        return jnp.transpose(state, (0, 2, 1))

    def migrate(payload):
        def branch(rank):
            stops = [(rank - 1) % N_EP, rank, (rank - 1 - N_EP // 2) % N_EP, (rank - 1) % N_EP]
            pairs = [(stops[0], stops[1]), (stops[2], stops[3]), (stops[1], stops[2])]
            return lambda block: lax.ppermute(block, "ep", pairs)

        return lax.switch(root, [branch(rank) for rank in range(N_EP)], payload)

    def settle(states, arrived):
        out = []
        for number, state in enumerate(states):
            fresh = arrived[:, number * hidden : (number + 1) * hidden]
            out.append([jnp.where(mine[n], fresh, state[n]) for n in range(local_count)])
        return out

    def payload_of(states):
        return jnp.concatenate([jnp.where(moved == 1, state[1], state[0]) for state in states], axis=1)

    weights = [gate_w, side(down_w)]
    moments = [gate_m, gate_v, side(down_m), side(down_v)]
    gate_now, down_now = settle(weights, migrate(payload_of(weights)))
    block = jnp.concatenate(gate_now + down_now, axis=1)

    half = shard // 2
    z_left, z_right = send(block, Z_UP), send(block, Z_DOWN)
    far = jnp.concatenate([send(z_left[:half], Z_UP), send(z_right[half:], Z_DOWN)], axis=0)
    near = [jnp.where(zb == 1, z_left, z_right), jnp.where(zb == 1, z_right, z_left)]

    def gather_x(piece):
        own = jnp.concatenate(spread(piece, X_UP, X_DOWN), axis=0)
        return [own, send(own, CORE)]

    own_parts = gather_x(block)
    near_parts = gather_x(near[0]) + gather_x(near[1])
    own_parts = own_parts + gather_x(far)
    cut = local_count * hidden
    gate_full = [jnp.concatenate([p[:, :cut] for p in parts], axis=0) for parts in (own_parts, near_parts)]
    down_full = [jnp.concatenate([p[:, cut:] for p in parts], axis=0) for parts in (own_parts, near_parts)]

    tokens_here = to_relative(tokens, x, zh, c)
    grads_here = to_relative(grad_out, x, zh, c)
    tokens_pair, grads_pair = send(tokens_here, Z_PAIR), send(grads_here, Z_PAIR)

    def gather_y(piece):
        return jnp.concatenate(spread(piece, Y_UP, Y_DOWN), axis=0)

    tok = [gather_y(tokens_here), gather_y(tokens_pair)]
    grd = [gather_y(grads_here), gather_y(grads_pair)]

    inverse_new = jnp.sum(jnp.where(new_place[None, :] == slots[:, None], slots[None, :], 0), axis=1)
    new_slot = jnp.sum(jnp.where(routes[:, :, None] == slots, inverse_new, 0), axis=2)
    hits = new_slot[:, :, None] == slots
    by_slot = jnp.sum(jnp.where(hits, probs[:, :, None], 0.0), axis=1)
    all_probs = lax.all_gather(by_slot, "ep", axis=0)
    spans = []
    for other in (0, 1):
        zl_there = (zb ^ other) * 2 + za
        spans.append((y * N_ZL + zl_there) * local_count)
    own_probs = []
    for pair in (0, 1):
        rows = []
        for step in (0, -1, 1, 2):
            rank = (y + step) % N_Y * N_ZL + zb * 2 + (za ^ pair)
            rows.append(lax.dynamic_index_in_dim(all_probs, rank, 0, keepdims=False))
        rows = jnp.concatenate(rows, axis=0)
        own_probs.append([lax.dynamic_slice_in_dim(rows, span, local_count, axis=1) for span in spans])

    def wide(table):
        return jnp.concatenate(
            [jnp.broadcast_to(table[:, n : n + 1], (table.shape[0], hidden)) for n in range(local_count)], axis=1
        )

    weighted, slopes, dots = {}, {}, {}
    for pair in (0, 1):
        for who in (1, 0):
            pre = dot(tok[pair], gate_full[who])
            up = dot(grd[pair], down_full[who])
            scale = wide(own_probs[pair][who])
            sigmoid = jax.nn.sigmoid(pre)
            act = (pre * sigmoid).astype(BF16).astype(F32)
            weighted[pair, who] = (scale * act).astype(BF16)
            slopes[pair, who] = (scale * up * sigmoid * (1.0 + pre * (1.0 - sigmoid))).astype(BF16)
            dots[pair, who] = [
                jnp.sum((act * up)[:, n * hidden : (n + 1) * hidden], axis=1) for n in range(local_count)
            ]

    def scatter_y(rows):
        blocks = [rows[n * tok_rows : (n + 1) * tok_rows] for n in range(4)]
        own, left, right = collect(blocks, Y_UP, Y_DOWN)
        return own.astype(F32) + left.astype(F32) + right.astype(F32)

    mixed, back = [], []
    for pair in (0, 1):
        rows = dot(weighted[pair, 0], down_full[0], COLS) + dot(weighted[pair, 1], down_full[1], COLS)
        mixed.append(scatter_y(rows.astype(BF16)))
        rows = dot(slopes[pair, 0], gate_full[0], COLS) + dot(slopes[pair, 1], gate_full[1], COLS)
        back.append(scatter_y(rows.astype(BF16)))
    mixed = mixed[0] + send(mixed[1].astype(BF16), Z_PAIR).astype(F32)
    back = back[0] + send(back[1].astype(BF16), Z_PAIR).astype(F32)
    mixed = to_absolute(mixed.astype(BF16), x, zh, c)
    grad_tokens = to_absolute(back.astype(BF16), x, zh, c)

    table = jnp.zeros((N_EP, 2 * local_count, tok_rows), F32)
    for pair in (0, 1):
        entry = jnp.stack(dots[pair, 0] + dots[pair, 1], axis=0)
        for number, step in enumerate((0, -1, 1, 2)):
            rank = (y + step) % N_Y * N_ZL + zb * 2 + (za ^ pair)
            piece = entry[:, number * tok_rows : (number + 1) * tok_rows]
            table = lax.dynamic_update_slice_in_dim(table, piece[None], rank, 0)
    table = lax.all_to_all(table, "ep", split_axis=0, concat_axis=0, tiled=True)
    table = table.reshape(N_Y, 2, 2, 2, local_count, tok_rows)
    table = jnp.where(zb == 1, table[:, 1], table[:, 0])
    table = jnp.where(zb == 1, table[:, :, ::-1], table)
    table = jnp.transpose(table, (0, 2, 1, 3, 4)).reshape(experts, tok_rows)
    grad_probs = jnp.sum(jnp.where(hits, jnp.transpose(table)[:, None, :], 0.0), axis=2)

    def scatter_x(who):
        gate = dot(tok[0], slopes[0, who], ROWS) + dot(tok[1], slopes[1, who], ROWS)
        down = dot(grd[0], weighted[0, who], ROWS) + dot(grd[1], weighted[1, who], ROWS)
        part = jnp.concatenate([gate, down], axis=1).astype(BF16)
        rows = N_X * shard
        out = []
        for n in range(N_ZH):
            ours = part[2 * n * rows : (2 * n + 1) * rows]
            theirs = part[(2 * n + 1) * rows : (2 * n + 2) * rows]
            total = add(ours, send(theirs, CORE))
            own, left, right = collect([total[i * shard : (i + 1) * shard] for i in range(4)], X_UP, X_DOWN)
            out.append(own.astype(F32) + left.astype(F32) + right.astype(F32))
        return out

    near_grads = scatter_x(1)
    own_grads = scatter_x(0)
    to_right = jnp.where(zb == 1, near_grads[1], near_grads[0])
    to_left = jnp.where(zb == 1, near_grads[0], near_grads[1])
    distant = own_grads[1].astype(BF16)
    from_left, from_right = send(distant[:half], Z_UP), send(distant[half:], Z_DOWN)
    to_right = jnp.concatenate([to_right[:half] + from_left.astype(F32), to_right[half:]], axis=0).astype(BF16)
    to_left = jnp.concatenate([to_left[:half], to_left[half:] + from_right.astype(F32)], axis=0).astype(BF16)
    grad = own_grads[0] + send(to_right, Z_UP).astype(F32) + send(to_left, Z_DOWN).astype(F32)

    gate_m_now, gate_v_now, down_m_now, down_v_now = settle(moments, migrate(payload_of(moments)))
    gate_next, down_next = [], []
    for n in range(local_count):
        piece = grad[:, n * hidden : (n + 1) * hidden]
        gate_next.append(adam_update(gate_now[n], gate_m_now[n], gate_v_now[n], piece))
        piece = grad[:, (local_count + n) * hidden : (local_count + n + 1) * hidden]
        done = adam_update(down_now[n], down_m_now[n], down_v_now[n], piece)
        down_next.append([jnp.transpose(entry) for entry in done])
    stacked = [jnp.stack([entry[i] for entry in gate_next], axis=0) for i in range(3)]
    stacked += [jnp.stack([entry[i] for entry in down_next], axis=0) for i in range(3)]
    return (mixed, grad_tokens, grad_probs, *stacked)


def solution(mesh):
    tok = P(("ep", "dp"), None)
    gate, down = P("ep", "dp", None), P("ep", None, "dp")
    in_specs = (tok, tok, tok, tok, P(), P(), gate, gate, gate, down, down, down)
    out_specs = (tok, tok, tok, gate, gate, gate, down, down, down)
    return jax.shard_map(per_device, mesh=mesh, in_specs=in_specs, out_specs=out_specs, check_vma=False)
```

time: 963 us -> 734 us (0.76)
  waiting for transfers between devices: 682 us -> 168 us
  starting transfers between devices: 31.6 us -> 212 us
  matrix products: 39.2 us -> 131 us
  blocking collectives: 0 us -> 33.2 us
  between operations: 31.1 us -> 4.66 us
  local copies, waits for them, and re-layouts: 105 us -> 119 us
  other arithmetic: 63.9 us -> 52 us
    psum x1 -> x0, waiting for transfers between devices: 215 us -> none  [from_root(): return lax.psum(block, axis)]
    ppermute x0 -> x86, starting transfers between devices: none -> 201 us  [the longest x84 200 us: send(): return lax.ppermute(block, BOTH, pairs)]
    all_to_all x4 -> x1, waiting for transfers between devices: 202 us -> 6.26 us  [per_device(): table = lax.all_to_all(table, 'ep', split_axis=0, concat_axis=0, tiled=True)]
    ppermute x0 -> x86, waiting for transfers between devices: none -> 161 us  [the longest x84 161 us: send(): return lax.ppermute(block, BOTH, pairs)]
    all_gather x4 -> x0, waiting for transfers between devices: 140 us -> none  [the longest x2 82.9 us: run_forward(): lax.all_gather(current[0][local_index], 'dp', axis=0, tiled=True)]
    unnamed x9 -> x0, waiting for transfers between devices: 126 us -> none
    dot_general x12 -> x24, matrix products: 39.2 us -> 131 us  [dot(): lax.dot_general(left, right, (dims, ((), ())), preferred_element_type=F32)]
    gather x5 -> x0, local copies, waits for them, and re-layouts: 41.3 us -> none  [the longest x1 12.1 us: per_device(): back_rows.reshape(capacity, width)[position]]
  transfers between devices with their start and end apart: 11 -> 87, of which waited for: 7 -> 26; matrix products, arithmetic and copies ran while one was open for 15% -> 29% of each run, Pallas kernels for 0% -> 0%
where the time goes in v1:
time: 734 us; the launch traced here: 720 us
  starting transfers between devices  212 us (29%)
  waiting for transfers between devices  168 us (23%)
  matrix products  131 us (18%)
  local copies, waits for them, and re-layouts  119 us (16%)
  other arithmetic  52 us (7%)
  blocking collectives  33.2 us (5%)
    ppermute x84, starting transfers between devices, send(): return lax.ppermute(block, BOTH, pairs)  200 us
    ppermute x84, waiting for transfers between devices, send(): return lax.ppermute(block, BOTH, pairs)  161 us
    dot_general x24, matrix products, dot(): lax.dot_general(left, right, (dims, ((), ())), preferred_element_type=F32)  131 us
    unnamed x320, local copies, waits for them, and re-layouts  51.6 us
    all_gather x1, blocking collectives, per_device(): all_probs = lax.all_gather(by_slot, 'ep', axis=0)  33.2 us
    concatenate x4, local copies, waits for them, and re-layouts, gather_x(): own = jnp.concatenate(spread(piece, X_UP, X_DOWN), axis=0)  19.4 us
    slice x8, local copies, waits for them, and re-layouts, per_device(): p[:, :cut]  16.7 us
  transfers between devices with their start and end apart: 87, of which 26 were waited for; matrix products, arithmetic and copies ran while one was open for 29% of the time, Pallas kernels for 0%

profile of v1, /device:TPU:33, one launch (start us, length us, event | category | flops | bytes accessed | tf_op | source)
XLA Modules:
  0.0 720.0 jit_solution(1302739520848406315)
XLA Ops:
  24.8 17.3 %collective-permute-start.41 = (bf16[128,2048]{0,1:T(8,128)(2,1)S(1)}, bf16[128,2048]{0,1:T(8,128)(2,1)}, u32[]{:S(2)}, u32[]{:S(2)}) collective-permute-start(bf16[128,2048]{0,1:T(8,128)(2,1)S(1)} %pad_maximum_fusion.10), channel_id=1, source_target_pairs={{0,32},{1,33},{2,34},{3,35},{4,36},{5,37},{6,38},{7,39},{8,40},{9,... | collective-permute-start | bytes 1572872 | tf_op jit(solution)/shard_map/ppermute | solution.py:42
  80.1 20.2 %collective-permute-start.74 = (bf16[128,2048]{1,0:T(8,128)(2,1)S(1)}, bf16[128,2048]{1,0:T(8,128)(2,1)S(1)}, u32[]{:S(2)}, u32[]{:S(2)}) collective-permute-start(bf16[128,2048]{1,0:T(8,128)(2,1)S(1)} %copy-done.119), channel_id=1, source_target_pairs={{0,64},{1,65},{2,66},{3,67},{4,68},{5,69},{6,70},{7,71},{8,72},{9,... | collective-permute-start | bytes 1572872 | tf_op jit(solution)/shard_map/ppermute | solution.py:42
  155.9 16.3 %collective-permute-start.40 = (bf16[512,2048]{0,1:T(8,128)(2,1)S(1)}, bf16[512,2048]{0,1:T(8,128)(2,1)}, u32[]{:S(2)}, u32[]{:S(2)}) collective-permute-start(bf16[512,2048]{0,1:T(8,128)(2,1)S(1)} %concatenate.245), channel_id=1, source_target_pairs={{0,1},{1,0},{2,3},{3,2},{4,5},{5,4},{6,7},{7,6},{8,9},{9,8},{10,11... | collective-permute-start | bytes 6291464 | tf_op jit(solution)/shard_map/ppermute | solution.py:42
  220.7 10.0 %collective-permute-done.47 = bf16[64,2048]{0,1:T(8,128)(2,1)S(1)} collective-permute-done((bf16[64,2048]{0,1:T(8,128)(2,1)}, bf16[64,2048]{0,1:T(8,128)(2,1)S(1)}, u32[]{:S(2)}, u32[]{:S(2)}) %collective-permute-start.47) | collective-permute-done | bytes 262176 | tf_op jit(solution)/shard_map/ppermute | solution.py:42
  291.2 10.3 %all-to-all-start = ((f32[16,4,128]{2,1,0:T(4,128)}), f32[16,4,128]{2,1,0:T(4,128)S(1)}, u32[]{:S(2)}, u32[]{:S(2)}) async-start(f32[16,4,128]{2,1,0:T(4,128)} %constant_dynamic-update-slice_fusion.114), calls=%async_computation | async-start | bytes 65536 | tf_op jit(solution)/shard_map/all_to_all | solution.py:250
  308.5 33.2 %all-gather = f32[2048,32]{0,1:T(8,128)S(1)} all-gather(f32[128,32]{0,1:T(8,128)S(1)} %get-tuple-element.153), channel_id=2, replica_groups=mesh['ep'=16,'dp'=16] {'ep'}, dimensions={0}, use_global_device_ids=true | all-gather | bytes 278528 | tf_op jit(solution)/shard_map/all_gather | solution.py:194
  348.4 7.6 %fusion.30 = f32[2048,1024]{0,1:T(8,128)} fusion(bf16[512,2048]{1,0:T(8,128)(2,1)} %constant_dynamic-update-slice_fusion.93, f32[512,512]{1,0:T(8,128)S(1)} %broadcast_in_dim.167, f32[512,512]{1,0:T(8,128)S(1)} %broadcast_in_dim.165, f32[512,1024]{1,0:T(8,128)S(1)} %copy-done.4), kind=kOutput, calls=%fused_computation.108 | convolution fusion | flops 2152202240 | bytes 14680064 | tf_op jit(solution)/shard_map/dot_general | solution.py:113
  370.4 7.5 %fusion.34 = f32[2048,1024]{0,1:T(8,128)} fusion(bf16[512,2048]{1,0:T(8,128)(2,1)} %constant_dynamic-update-slice_fusion.93, f32[512,512]{1,0:T(8,128)S(1)} %broadcast_in_dim.163, f32[512,512]{1,0:T(8,128)S(1)} %broadcast_in_dim.161, f32[512,1024]{1,0:T(8,128)S(1)} %copy-done.129), kind=kOutput, calls=%fused_computation.110 | convolution fusion | flops 2152202240 | bytes 14680064 | tf_op jit(solution)/shard_map/dot_general | solution.py:113
  403.1 8.0 %fusion.133 = f32[2048,1024]{0,1:T(8,128)} fusion(bf16[512,2048]{1,0:T(8,128)(2,1)S(1)} %copy-done.102, f32[512,1024]{1,0:T(8,128)} %get-tuple-element.517, f32[512,512]{1,0:T(8,128)S(1)} %broadcast_in_dim.163, f32[512,512]{1,0:T(8,128)S(1)} %broadcast_in_dim.161, f32[512,1024]{1,0:T(8,128)S(1)} %copy-done.130), kind=kOutput, calls=%fused_computation.547 | convolution fusion | flops 2153250816 | bytes 16777216 | tf_op jit(solution)/shard_map/dot_general | solution.py:113
  417.9 18.9 %collective-permute-start.87 = (bf16[64,2048]{1,0:T(8,128)(2,1)}, bf16[64,2048]{1,0:T(8,128)(2,1)}, u32[]{:S(2)}, u32[]{:S(2)}) collective-permute-start(bf16[64,2048]{1,0:T(8,128)(2,1)} %get-tuple-element.432), channel_id=1, source_target_pairs={{0,64},{1,65},{2,66},{3,67},{4,68},{5,69},{6,70},{7,71},{8,72},{9,... | collective-permute-start | bytes 786440 | tf_op jit(solution)/shard_map/ppermute | solution.py:42
  462.7 7.0 add_convert_fusion.3
  469.7 7.1 add_convert_fusion.2
  482.3 11.8 %collective-permute-start.89 = (bf16[64,2048]{1,0:T(8,128)(2,1)S(1)}, bf16[64,2048]{1,0:T(8,128)(2,1)S(1)}, u32[]{:S(2)}, u32[]{:S(2)}) collective-permute-start(bf16[64,2048]{1,0:T(8,128)(2,1)S(1)} %copy-done.95), channel_id=1, source_target_pairs={{0,192},{1,193},{2,194},{3,195},{4,196},{5,197},{6,198},{7,199},{8... | collective-permute-start | bytes 786440 | tf_op jit(solution)/shard_map/ppermute | solution.py:42
  509.1 9.6 %collective-permute-done.72 = bf16[128,2048]{1,0:T(8,128)(2,1)S(1)} collective-permute-done((bf16[128,2048]{1,0:T(8,128)(2,1)S(1)}, bf16[128,2048]{1,0:T(8,128)(2,1)S(1)}, u32[]{:S(2)}, u32[]{:S(2)}) %collective-permute-start.72) | collective-permute-done | bytes 524320 | tf_op jit(solution)/shard_map/ppermute | solution.py:42
  520.3 20.8 %collective-permute-done.90 = bf16[128,2048]{1,0:T(8,128)(2,1)S(1)} collective-permute-done((bf16[128,2048]{1,0:T(8,128)(2,1)S(1)}, bf16[128,2048]{1,0:T(8,128)(2,1)S(1)}, u32[]{:S(2)}, u32[]{:S(2)}) %collective-permute-start.90) | collective-permute-done | bytes 524320 | tf_op jit(solution)/shard_map/ppermute | solution.py:42
  545.4 10.3 %collective-permute-done.81 = bf16[128,2048]{1,0:T(8,128)(2,1)S(1)} collective-permute-done((bf16[128,2048]{1,0:T(8,128)(2,1)S(1)}, bf16[128,2048]{1,0:T(8,128)(2,1)S(1)}, u32[]{:S(2)}, u32[]{:S(2)}) %collective-permute-start.81) | collective-permute-done | bytes 524320 | tf_op jit(solution)/shard_map/ppermute | solution.py:42
  580.2 9.1 %collective-permute-done.103 = bf16[64,2048]{0,1:T(8,128)(2,1)S(1)} collective-permute-done((bf16[64,2048]{0,1:T(8,128)(2,1)S(1)}, bf16[64,2048]{0,1:T(8,128)(2,1)S(1)}, u32[]{:S(2)}, u32[]{:S(2)}) %collective-permute-start.103) | collective-permute-done | bytes 262176 | tf_op jit(solution)/shard_map/ppermute | solution.py:42
  592.6 7.9 %collective-permute-done.108 = bf16[64,2048]{0,1:T(8,128)(2,1)S(1)} collective-permute-done((bf16[64,2048]{0,1:T(8,128)(2,1)S(1)}, bf16[64,2048]{0,1:T(8,128)(2,1)S(1)}, u32[]{:S(2)}, u32[]{:S(2)}) %collective-permute-start.108) | collective-permute-done | bytes 262176 | tf_op jit(solution)/shard_map/ppermute | solution.py:42
  604.2 7.6 %collective-permute-done.93 = bf16[64,2048]{0,1:T(8,128)(2,1)S(1)} collective-permute-done((bf16[64,2048]{0,1:T(8,128)(2,1)S(1)}, bf16[64,2048]{0,1:T(8,128)(2,1)S(1)}, u32[]{:S(2)}, u32[]{:S(2)}) %collective-permute-start.93) | collective-permute-done | bytes 262176 | tf_op jit(solution)/shard_map/ppermute | solution.py:42
  611.8 10.2 %collective-permute-start.111 = (bf16[128,2048]{0,1:T(8,128)(2,1)S(1)}, bf16[128,2048]{0,1:T(8,128)(2,1)S(1)}, u32[]{:S(2)}, u32[]{:S(2)}) collective-permute-start(bf16[128,2048]{0,1:T(8,128)(2,1)S(1)} %pad_maximum_fusion.28), channel_id=1, source_target_pairs={{0,12},{1,13},{2,14},{3,15},{4,0},{5,1},{6,2},{7,3},{8,4},{9,5},{1... | collective-permute-start | bytes 1572872 | tf_op jit(solution)/shard_map/ppermute | solution.py:42
  624.5 20.7 %collective-permute-done.111 = bf16[128,2048]{0,1:T(8,128)(2,1)S(1)} collective-permute-done((bf16[128,2048]{0,1:T(8,128)(2,1)S(1)}, bf16[128,2048]{0,1:T(8,128)(2,1)S(1)}, u32[]{:S(2)}, u32[]{:S(2)}) %collective-permute-start.111) | collective-permute-done | bytes 524320 | tf_op jit(solution)/shard_map/ppermute | solution.py:42
  668.1 8.0 %collective-permute-start.115 = (bf16[128,2048]{0,1:T(8,128)(2,1)S(1)}, bf16[128,2048]{0,1:T(8,128)(2,1)S(1)}, u32[]{:S(2)}, u32[]{:S(2)}) collective-permute-start(bf16[128,2048]{0,1:T(8,128)(2,1)S(1)} %pad_maximum_fusion.30), channel_id=1, source_target_pairs={{0,34},{1,35},{2,32},{3,33},{4,38},{5,39},{6,36},{7,37},{8,42},{9,... | collective-permute-start | bytes 1572872 | tf_op jit(solution)/shard_map/ppermute | solution.py:42
  676.1 11.7 %collective-permute-done.112 = bf16[64,2048]{0,1:T(8,128)(2,1)S(1)} collective-permute-done((bf16[64,2048]{0,1:T(8,128)(2,1)S(1)}, bf16[64,2048]{0,1:T(8,128)(2,1)S(1)}, u32[]{:S(2)}, u32[]{:S(2)}) %collective-permute-start.112) | collective-permute-done | bytes 262176 | tf_op jit(solution)/shard_map/ppermute | solution.py:42
  689.9 21.1 %collective-permute-done.113 = bf16[128,2048]{0,1:T(8,128)(2,1)S(1)} collective-permute-done((bf16[128,2048]{0,1:T(8,128)(2,1)S(1)}, bf16[128,2048]{0,1:T(8,128)(2,1)S(1)}, u32[]{:S(2)}, u32[]{:S(2)}) %collective-permute-start.113) | collective-permute-done | bytes 524320 | tf_op jit(solution)/shard_map/ppermute | solution.py:42
  (707 shorter events, 409.9 us)
Async XLA Ops:
  13.4 88.8 %collective-permute-start.32 = (bf16[128,2048]{1,0:T(8,128)(2,1)}, bf16[128,2048]{1,0:T(8,128)(2,1)S(1)}, u32[]{:S(2)}, u32[]{:S(2)}) collective-permute-start(bf16[128,2048]{1,0:T(8,128)(2,1)} %get-tuple-element.196), channel_id=1, source_target_pairs={{0,64},{1,65},{2,66},{3,67},{4,68},{5,69},{6,70},{7,71},{8,72},{9,... | collective-permute-start | bytes 1572872 | tf_op jit(solution)/shard_map/ppermute | solution.py:42
  14.7 88.4 %collective-permute-start.33 = (bf16[128,2048]{1,0:T(8,128)(2,1)}, bf16[128,2048]{1,0:T(8,128)(2,1)S(1)}, u32[]{:S(2)}, u32[]{:S(2)}) collective-permute-start(bf16[128,2048]{1,0:T(8,128)(2,1)} %get-tuple-element.196), channel_id=1, source_target_pairs={{0,192},{1,193},{2,194},{3,195},{4,196},{5,197},{6,198},{7,199},{8... | collective-permute-start | bytes 1572872 | tf_op jit(solution)/shard_map/ppermute | solution.py:42
  24.8 50.7 %collective-permute-start.41 = (bf16[128,2048]{0,1:T(8,128)(2,1)S(1)}, bf16[128,2048]{0,1:T(8,128)(2,1)}, u32[]{:S(2)}, u32[]{:S(2)}) collective-permute-start(bf16[128,2048]{0,1:T(8,128)(2,1)S(1)} %pad_maximum_fusion.10), channel_id=1, source_target_pairs={{0,32},{1,33},{2,34},{3,35},{4,36},{5,37},{6,38},{7,39},{8,40},{9,... | collective-permute-start | bytes 1572872 | tf_op jit(solution)/shard_map/ppermute | solution.py:42
  42.1 34.7 %collective-permute-start.43 = (bf16[128,2048]{0,1:T(8,128)(2,1)S(1)}, bf16[128,2048]{0,1:T(8,128)(2,1)S(1)}, u32[]{:S(2)}, u32[]{:S(2)}) collective-permute-start(bf16[128,2048]{0,1:T(8,128)(2,1)S(1)} %pad_maximum_fusion.10), channel_id=1, source_target_pairs={{0,34},{1,35},{2,32},{3,33},{4,38},{5,39},{6,36},{7,37},{8,42},{9,... | collective-permute-start | bytes 1572872 | tf_op jit(solution)/shard_map/ppermute | solution.py:42
  75.5 33.3 %collective-permute-start.36 = (bf16[128,2048]{0,1:T(8,128)(2,1)S(1)}, bf16[128,2048]{0,1:T(8,128)(2,1)S(1)}, u32[]{:S(2)}, u32[]{:S(2)}) collective-permute-start(bf16[128,2048]{0,1:T(8,128)(2,1)S(1)} %pad_maximum_fusion.10), channel_id=1, source_target_pairs={{0,4},{1,5},{2,6},{3,7},{4,8},{5,9},{6,10},{7,11},{8,12},{9,13},{1... | collective-permute-start | bytes 1572872 | tf_op jit(solution)/shard_map/ppermute | solution.py:42
  155.9 84.2 %collective-permute-start.40 = (bf16[512,2048]{0,1:T(8,128)(2,1)S(1)}, bf16[512,2048]{0,1:T(8,128)(2,1)}, u32[]{:S(2)}, u32[]{:S(2)}) collective-permute-start(bf16[512,2048]{0,1:T(8,128)(2,1)S(1)} %concatenate.245), channel_id=1, source_target_pairs={{0,1},{1,0},{2,3},{3,2},{4,5},{5,4},{6,7},{7,6},{8,9},{9,8},{10,11... | collective-permute-start | bytes 6291464 | tf_op jit(solution)/shard_map/ppermute | solution.py:42
  189.5 53.0 %collective-permute-start.59 = (bf16[512,2048]{0,1:T(8,128)(2,1)}, bf16[512,2048]{0,1:T(8,128)(2,1)}, u32[]{:S(2)}, u32[]{:S(2)}) collective-permute-start(bf16[512,2048]{0,1:T(8,128)(2,1)} %concatenate.252), channel_id=1, source_target_pairs={{0,1},{1,0},{2,3},{3,2},{4,5},{5,4},{6,7},{7,6},{8,9},{9,8},{10,11... | collective-permute-start | bytes 6291464 | tf_op jit(solution)/shard_map/ppermute | solution.py:42
  203.0 42.0 %collective-permute-start.54 = (bf16[512,2048]{0,1:T(8,128)(2,1)}, bf16[512,2048]{0,1:T(8,128)(2,1)}, u32[]{:S(2)}, u32[]{:S(2)}) collective-permute-start(bf16[512,2048]{0,1:T(8,128)(2,1)} %concatenate.251), channel_id=1, source_target_pairs={{0,1},{1,0},{2,3},{3,2},{4,5},{5,4},{6,7},{7,6},{8,9},{9,8},{10,11... | collective-permute-start | bytes 6291464 | tf_op jit(solution)/shard_map/ppermute | solution.py:42
  383.5 98.5 %collective-permute-start.69 = (bf16[64,2048]{1,0:T(8,128)(2,1)}, bf16[64,2048]{1,0:T(8,128)(2,1)}, u32[]{:S(2)}, u32[]{:S(2)}) collective-permute-start(bf16[64,2048]{1,0:T(8,128)(2,1)} %get-tuple-element.444), channel_id=1, source_target_pairs={{0,64},{1,65},{2,66},{3,67},{4,68},{5,69},{6,70},{7,71},{8,72},{9,... | collective-permute-start | bytes 786440 | tf_op jit(solution)/shard_map/ppermute | solution.py:42
  383.5 110.7 %collective-permute-start.71 = (bf16[64,2048]{1,0:T(8,128)(2,1)}, bf16[64,2048]{1,0:T(8,128)(2,1)}, u32[]{:S(2)}, u32[]{:S(2)}) collective-permute-start(bf16[64,2048]{1,0:T(8,128)(2,1)} %get-tuple-element.445), channel_id=1, source_target_pairs={{0,192},{1,193},{2,194},{3,195},{4,196},{5,197},{6,198},{7,199},{8... | collective-permute-start | bytes 786440 | tf_op jit(solution)/shard_map/ppermute | solution.py:42
  400.4 96.3 %collective-permute-start.60 = (bf16[64,2048]{1,0:T(8,128)(2,1)}, bf16[64,2048]{1,0:T(8,128)(2,1)}, u32[]{:S(2)}, u32[]{:S(2)}) collective-permute-start(bf16[64,2048]{1,0:T(8,128)(2,1)} %get-tuple-element.438), channel_id=1, source_target_pairs={{0,64},{1,65},{2,66},{3,67},{4,68},{5,69},{6,70},{7,71},{8,72},{9,... | collective-permute-start | bytes 786440 | tf_op jit(solution)/shard_map/ppermute | solution.py:42
  400.4 97.8 %collective-permute-start.62 = (bf16[64,2048]{1,0:T(8,128)(2,1)}, bf16[64,2048]{1,0:T(8,128)(2,1)}, u32[]{:S(2)}, u32[]{:S(2)}) collective-permute-start(bf16[64,2048]{1,0:T(8,128)(2,1)} %get-tuple-element.439), channel_id=1, source_target_pairs={{0,192},{1,193},{2,194},{3,195},{4,196},{5,197},{6,198},{7,199},{8... | collective-permute-start | bytes 786440 | tf_op jit(solution)/shard_map/ppermute | solution.py:42
  417.9 83.0 %collective-permute-start.87 = (bf16[64,2048]{1,0:T(8,128)(2,1)}, bf16[64,2048]{1,0:T(8,128)(2,1)}, u32[]{:S(2)}, u32[]{:S(2)}) collective-permute-start(bf16[64,2048]{1,0:T(8,128)(2,1)} %get-tuple-element.432), channel_id=1, source_target_pairs={{0,64},{1,65},{2,66},{3,67},{4,68},{5,69},{6,70},{7,71},{8,72},{9,... | collective-permute-start | bytes 786440 | tf_op jit(solution)/shard_map/ppermute | solution.py:42
  501.8 40.8 %collective-permute-start.63 = (bf16[128,2048]{1,0:T(8,128)(2,1)S(1)}, bf16[128,2048]{1,0:T(8,128)(2,1)S(1)}, u32[]{:S(2)}, u32[]{:S(2)}) collective-permute-start(bf16[128,2048]{1,0:T(8,128)(2,1)S(1)} %pad_maximum_fusion.13), channel_id=1, source_target_pairs={{0,192},{1,193},{2,194},{3,195},{4,196},{5,197},{6,198},{7,199},{8... | collective-permute-start | bytes 1572872 | tf_op jit(solution)/shard_map/ppermute | solution.py:42
  504.9 39.3 %collective-permute-start.61 = (bf16[128,2048]{1,0:T(8,128)(2,1)S(1)}, bf16[128,2048]{1,0:T(8,128)(2,1)S(1)}, u32[]{:S(2)}, u32[]{:S(2)}) collective-permute-start(bf16[128,2048]{1,0:T(8,128)(2,1)S(1)} %pad_maximum_fusion.12), channel_id=1, source_target_pairs={{0,64},{1,65},{2,66},{3,67},{4,68},{5,69},{6,70},{7,71},{8,72},{9,... | collective-permute-start | bytes 1572872 | tf_op jit(solution)/shard_map/ppermute | solution.py:42
  507.4 33.7 %collective-permute-start.90 = (bf16[128,2048]{1,0:T(8,128)(2,1)S(1)}, bf16[128,2048]{1,0:T(8,128)(2,1)S(1)}, u32[]{:S(2)}, u32[]{:S(2)}) collective-permute-start(bf16[128,2048]{1,0:T(8,128)(2,1)S(1)} %pad_maximum_fusion.19), channel_id=1, source_target_pairs={{0,192},{1,193},{2,194},{3,195},{4,196},{5,197},{6,198},{7,199},{8... | collective-permute-start | bytes 1572872 | tf_op jit(solution)/shard_map/ppermute | solution.py:42
  579.3 32.5 %collective-permute-start.93 = (bf16[64,2048]{0,1:T(8,128)(2,1)S(1)}, bf16[64,2048]{0,1:T(8,128)(2,1)S(1)}, u32[]{:S(2)}, u32[]{:S(2)}) collective-permute-start(bf16[64,2048]{0,1:T(8,128)(2,1)S(1)} %get-tuple-element.402), channel_id=1, source_target_pairs={{0,4},{1,5},{2,6},{3,7},{4,8},{5,9},{6,10},{7,11},{8,12},{9,13},{1... | collective-permute-start | bytes 786440 | tf_op jit(solution)/shard_map/ppermute | solution.py:42
  589.3 32.7 %collective-permute-start.95 = (bf16[64,2048]{0,1:T(8,128)(2,1)S(1)}, bf16[64,2048]{0,1:T(8,128)(2,1)S(1)}, u32[]{:S(2)}, u32[]{:S(2)}) collective-permute-start(bf16[64,2048]{0,1:T(8,128)(2,1)S(1)} %get-tuple-element.403), channel_id=1, source_target_pairs={{0,12},{1,13},{2,14},{3,15},{4,0},{5,1},{6,2},{7,3},{8,4},{9,5},{1... | collective-permute-start | bytes 786440 | tf_op jit(solution)/shard_map/ppermute | solution.py:42
  590.5 58.0 %collective-permute-start.101 = (bf16[128,2048]{0,1:T(8,128)(2,1)S(1)}, bf16[128,2048]{0,1:T(8,128)(2,1)S(1)}, u32[]{:S(2)}, u32[]{:S(2)}) collective-permute-start(bf16[128,2048]{0,1:T(8,128)(2,1)S(1)} %pad_maximum_fusion.24), channel_id=1, source_target_pairs={{0,12},{1,13},{2,14},{3,15},{4,0},{5,1},{6,2},{7,3},{8,4},{9,5},{1... | collective-permute-start | bytes 1572872 | tf_op jit(solution)/shard_map/ppermute | solution.py:42
  600.5 48.1 %collective-permute-start.99 = (bf16[128,2048]{0,1:T(8,128)(2,1)S(1)}, bf16[128,2048]{0,1:T(8,128)(2,1)S(1)}, u32[]{:S(2)}, u32[]{:S(2)}) collective-permute-start(bf16[128,2048]{0,1:T(8,128)(2,1)S(1)} %pad_maximum_fusion.23), channel_id=1, source_target_pairs={{0,4},{1,5},{2,6},{3,7},{4,8},{5,9},{6,10},{7,11},{8,12},{9,13},{1... | collective-permute-start | bytes 1572872 | tf_op jit(solution)/shard_map/ppermute | solution.py:42
  600.5 52.1 %collective-permute-start.106 = (bf16[128,2048]{0,1:T(8,128)(2,1)S(1)}, bf16[128,2048]{0,1:T(8,128)(2,1)S(1)}, u32[]{:S(2)}, u32[]{:S(2)}) collective-permute-start(bf16[128,2048]{0,1:T(8,128)(2,1)S(1)} %pad_maximum_fusion.26), channel_id=1, source_target_pairs={{0,12},{1,13},{2,14},{3,15},{4,0},{5,1},{6,2},{7,3},{8,4},{9,5},{1... | collective-permute-start | bytes 1572872 | tf_op jit(solution)/shard_map/ppermute | solution.py:42
  611.8 33.4 %collective-permute-start.111 = (bf16[128,2048]{0,1:T(8,128)(2,1)S(1)}, bf16[128,2048]{0,1:T(8,128)(2,1)S(1)}, u32[]{:S(2)}, u32[]{:S(2)}) collective-permute-start(bf16[128,2048]{0,1:T(8,128)(2,1)S(1)} %pad_maximum_fusion.28), channel_id=1, source_target_pairs={{0,12},{1,13},{2,14},{3,15},{4,0},{5,1},{6,2},{7,3},{8,4},{9,5},{1... | collective-permute-start | bytes 1572872 | tf_op jit(solution)/shard_map/ppermute | solution.py:42
  646.3 43.6 %collective-permute-start.96 = (bf16[128,2048]{0,1:T(8,128)(2,1)S(1)}, bf16[128,2048]{0,1:T(8,128)(2,1)S(1)}, u32[]{:S(2)}, u32[]{:S(2)}) collective-permute-start(bf16[128,2048]{0,1:T(8,128)(2,1)S(1)} %pad_maximum_fusion.22), channel_id=1, source_target_pairs={{0,12},{1,13},{2,14},{3,15},{4,0},{5,1},{6,2},{7,3},{8,4},{9,5},{1... | collective-permute-start | bytes 1572872 | tf_op jit(solution)/shard_map/ppermute | solution.py:42
  648.5 41.4 %collective-permute-start.94 = (bf16[128,2048]{0,1:T(8,128)(2,1)S(1)}, bf16[128,2048]{0,1:T(8,128)(2,1)S(1)}, u32[]{:S(2)}, u32[]{:S(2)}) collective-permute-start(bf16[128,2048]{0,1:T(8,128)(2,1)S(1)} %pad_maximum_fusion.21), channel_id=1, source_target_pairs={{0,4},{1,5},{2,6},{3,7},{4,8},{5,9},{6,10},{7,11},{8,12},{9,13},{1... | collective-permute-start | bytes 1572872 | tf_op jit(solution)/shard_map/ppermute | solution.py:42
  (195 other events, 2572.6 us)
